TPU v7x, 32 devices: a whole 2x2x4 slice. The times are simulated.
32 devices in a mesh: doc: 4 (over z), ctx: 8 (over y, x, core).
Axes of the slice: x: 2, y: 2, z: 4, core: 2. Of those that a mesh axis runs over, the one named last changes fastest.
Arguments:
- queries: bfloat16 [4, 1024, 4096], P('doc', 'ctx'), may hold values from -6 to 6
- out_grad: bfloat16 [4, 1024, 4096], P('doc', 'ctx'), may hold values from -6 to 6
- mem_keys: bfloat16 [4, 64, 4096], P('doc', 'ctx'), may hold values from -6 to 6
- mem_values: bfloat16 [4, 64, 4096], P('doc', 'ctx'), may hold values from -6 to 6
Outputs:
- grad_queries: float32 [4, 1024, 4096], P('doc', 'ctx')
- grad_keys: float32 [4, 64, 4096], P('doc', 'ctx')
- grad_values: float32 [4, 64, 4096], P('doc', 'ctx')
All inputs are finite; a program needn't handle non-finite values.
Results may differ from a plain program's by a relative error of at most 0.0011.
Values may be sent and summed in bfloat16 or wider, within the bound.
A program may use at most 64 MiB of HBM per device.

v0:
```python
import jax
import jax.numpy as jnp
from jax import lax
from jax.sharding import PartitionSpec as P

HD = 128


def heads_view(block):
    return block.reshape(block.shape[0], block.shape[1] // HD, HD)


def score_pair(q_block, g_block, k_rows, v_rows):
    scores = jnp.einsum("qhd,khd->hqk", q_block, k_rows, preferred_element_type=jnp.float32)
    expo = jnp.exp(scores * HD ** (-0.5))
    dprob = jnp.einsum("qhd,khd->hqk", g_block, v_rows, preferred_element_type=jnp.float32)
    return (expo, dprob)


def grads_from(q_block, g_block, k_rows, expo, dprob, norm, drift):
    high = lax.Precision.HIGHEST
    scale = HD ** (-0.5)
    prob = expo / norm[:, :, None]
    dscore = prob * (dprob - drift[:, :, None])
    grad_q = jnp.einsum("hqk,khd->qhd", dscore, k_rows.astype(jnp.float32), precision=high) * scale
    grad_k = jnp.einsum("hqk,qhd->khd", dscore, q_block.astype(jnp.float32), precision=high) * scale
    grad_v = jnp.einsum("hqk,qhd->khd", prob, g_block.astype(jnp.float32), precision=high)
    return (grad_q, grad_k, grad_v)


def shards(queries, out_grad, mem_keys, mem_values):
    q_heads, g_heads, k_heads, v_heads = (
        lax.all_to_all(queries, "ctx", split_axis=2, concat_axis=1, tiled=True),
        lax.all_to_all(out_grad, "ctx", split_axis=2, concat_axis=1, tiled=True),
        lax.all_to_all(mem_keys, "ctx", split_axis=2, concat_axis=1, tiled=True),
        lax.all_to_all(mem_values, "ctx", split_axis=2, concat_axis=1, tiled=True),
    )
    q_rows = heads_view(q_heads[0])
    g_rows = heads_view(g_heads[0])
    qlen, nheads = (q_rows.shape[0], q_rows.shape[1])
    mem_rows = k_heads.shape[1]
    width = nheads * HD
    ndoc = lax.axis_size("doc")
    total = ndoc * mem_rows
    block = min(qlen, 512)
    nblock = qlen // block
    q_blocks = q_rows.reshape(nblock, block, nheads, HD)
    g_blocks = g_rows.reshape(nblock, block, nheads, HD)

    def to_blocks(stat):
        return jnp.transpose(stat.reshape(nheads, nblock, block), (1, 0, 2))

    def from_blocks(stat):
        return jnp.transpose(stat, (1, 0, 2)).reshape(nheads, qlen)

    pieces = (
        lax.all_gather(k_heads[0], "doc", axis=0, tiled=True),
        lax.all_gather(v_heads[0], "doc", axis=0, tiled=True),
    )
    key_piece = heads_view(pieces[0])
    value_piece = heads_view(pieces[1])

    def one_block(items):
        expo, dprob = score_pair(items[0], items[1], key_piece, value_piece)
        return (jnp.sum(expo, axis=2), jnp.sum(expo * dprob, axis=2))

    sums, weighs = lax.map(one_block, (q_blocks, g_blocks))
    norm = from_blocks(sums)
    weigh = from_blocks(weighs)
    drift = weigh / norm
    norm_blocks = to_blocks(norm)
    drift_blocks = to_blocks(drift)
    pieces = (
        lax.all_gather(k_heads[0], "doc", axis=0, tiled=True),
        lax.all_gather(v_heads[0], "doc", axis=0, tiled=True),
    )
    add_key_piece = heads_view(pieces[0])
    add_value_piece = heads_view(pieces[1])
    count = add_key_piece.shape[0]

    def one_block(accum, items):
        expo, dprob = score_pair(items[0], items[1], add_key_piece, add_value_piece)
        grad_q, grad_k, grad_v = grads_from(
            items[0], items[1], add_key_piece, expo, dprob, items[2], items[3]
        )
        return ((accum[0] + grad_k, accum[1] + grad_v), grad_q)

    zero_piece = jnp.zeros((count, nheads, HD), jnp.float32)
    sums, grad_q = lax.scan(
        one_block, (zero_piece, zero_piece), (q_blocks, g_blocks, norm_blocks, drift_blocks)
    )
    keys_out = sums[0]
    values_out = sums[1]
    grad_q, keys_all, values_all = (grad_q.reshape(qlen, nheads, HD), keys_out, values_out)
    grad_k, grad_v = (
        lax.psum_scatter(keys_all.reshape(total, width), "doc", scatter_dimension=0, tiled=True),
        lax.psum_scatter(values_all.reshape(total, width), "doc", scatter_dimension=0, tiled=True),
    )
    grad_q = grad_q.reshape(qlen, width)
    return (
        lax.all_to_all(grad_q[None], "ctx", split_axis=1, concat_axis=2, tiled=True),
        lax.all_to_all(grad_k[None], "ctx", split_axis=1, concat_axis=2, tiled=True),
        lax.all_to_all(grad_v[None], "ctx", split_axis=1, concat_axis=2, tiled=True),
    )


def solution(mesh):
    placed = (
        P("doc", "ctx", None),
        P("doc", "ctx", None),
        P("doc", "ctx", None),
        P("doc", "ctx", None),
    )
    return jax.shard_map(
        shards,
        mesh=mesh,
        in_specs=placed,
        out_specs=(P("doc", "ctx", None), P("doc", "ctx", None), P("doc", "ctx", None)),
        check_vma=False,
    )
```

profile of v0, /device:TPU:0, one launch (start us, length us, event | category | flops | bytes accessed | tf_op | source)
XLA Modules:
  0.0 316.2 jit_solution(13624893849439572052)
XLA Ops:
  7.2 4.3 %copy.77 = bf16[1,8,4096]{1,0,2:T(2,128)(2,1)S(1)} copy(bf16[1,8,4096]{2,1,0:T(8,128)(2,1)} %param.10) | data formatting | bytes 131072 | tf_op args[2]
  11.9 22.4 %reduce.1 = bf16[4096,8]{1,0:T(8,128)(2,1)S(1)} reduce(bf16[4096,1,8]{2,1,0:T(2,128)(2,1)S(1)} %bitcast.151, bf16[]{:T(256)} %broadcast.40), dimensions={1}, to_apply=%bitcast.87.reduce_sub_computation | reduce | bytes 131074
  34.3 1.7 reshape.41
  36.0 5.2 %all-to-all-start.1 = ((bf16[8,2,2048]{2,1,0:T(2,128)(2,1)}), bf16[8,2,2048]{2,1,0:T(2,128)(2,1)S(1)}, u32[]{:S(2)}, u32[]{:S(2)}) async-start(bf16[8,2,2048]{2,1,0:T(2,128)(2,1)} %reshape.41), calls=%async_computation.1 | async-start | bytes 131072 | tf_op jit(solution)/shard_map/all_to_all | solution.py:35
  41.2 2.8 copy.83
  44.0 22.3 %reduce.3 = bf16[4096,8]{1,0:T(8,128)(2,1)S(1)} reduce(bf16[4096,1,8]{2,1,0:T(2,128)(2,1)S(1)} %bitcast.157, bf16[]{:T(256)} %broadcast.40), dimensions={1}, to_apply=%bitcast.91.reduce_sub_computation | reduce | bytes 131074
  66.3 1.7 reshape.45
  68.0 4.2 %all-to-all-start.3 = ((bf16[8,2,2048]{2,1,0:T(2,128)(2,1)}), bf16[8,2,2048]{2,1,0:T(2,128)(2,1)S(1)}, u32[]{:S(2)}, u32[]{:S(2)}) async-start(bf16[8,2,2048]{2,1,0:T(2,128)(2,1)} %reshape.45), calls=%async_computation.3 | async-start | bytes 131072 | tf_op jit(solution)/shard_map/all_to_all | solution.py:36
  72.2 5.0 %copy.75 = bf16[1,128,4096]{1,0,2:T(2,128)(2,1)S(1)} copy(bf16[1,128,4096]{2,1,0:T(8,128)(2,1)} %param.8) | data formatting | bytes 2097152 | tf_op args[0]
  77.2 22.3 %reduce = bf16[4096,128]{1,0:T(8,128)(2,1)S(1)} reduce(bf16[4096,1,128]{2,1,0:T(2,128)(2,1)S(1)} %bitcast.158, bf16[]{:T(256)} %broadcast.40), dimensions={1}, to_apply=%bitcast.85.reduce_sub_computation | reduce | bytes 2097154
  99.5 1.1 reshape.39
  100.6 4.2 %all-to-all-start = ((bf16[8,2,32768]{2,1,0:T(2,128)(2,1)}), bf16[8,2,32768]{2,1,0:T(2,128)(2,1)S(1)}, u32[]{:S(2)}, u32[]{:S(2)}) async-start(bf16[8,2,32768]{2,1,0:T(2,128)(2,1)} %reshape.39), calls=%async_computation | async-start | bytes 2097152 | tf_op jit(solution)/shard_map/all_to_all | solution.py:33
  104.8 5.0 %copy.81 = bf16[1,128,4096]{1,0,2:T(2,128)(2,1)S(1)} copy(bf16[1,128,4096]{2,1,0:T(8,128)(2,1)} %param.9) | data formatting | bytes 2097152 | tf_op args[1]
  109.8 23.3 %reduce.2 = bf16[4096,128]{1,0:T(8,128)(2,1)} reduce(bf16[4096,1,128]{2,1,0:T(2,128)(2,1)S(1)} %bitcast.152, bf16[]{:T(256)} %broadcast.40), dimensions={1}, to_apply=%bitcast.89.reduce_sub_computation | reduce | bytes 2097154
  133.2 2.1 reshape.43
  135.3 4.2 %all-to-all-start.2 = ((bf16[8,2,32768]{2,1,0:T(2,128)(2,1)}), bf16[8,2,32768]{2,1,0:T(2,128)(2,1)}, u32[]{:S(2)}, u32[]{:S(2)}) async-start(bf16[8,2,32768]{2,1,0:T(2,128)(2,1)} %reshape.43), calls=%async_computation.2 | async-start | bytes 2097152 | tf_op jit(solution)/shard_map/all_to_all | solution.py:34
  139.7 2.8 reshape.42
  142.5 1.9 copy.78
  144.4 14.5 %all_gather.8 = bf16[256,512]{1,0:T(8,128)(2,1)S(1)} all-gather(bf16[64,512]{1,0:T(8,128)(2,1)S(1)} %bitcast.169), channel_id=1, replica_groups=mesh['doc'=4,'ctx'=8] {'doc'}, dimensions={0}, use_global_device_ids=true | all-gather | bytes 327680 | tf_op jit(solution)/shard_map/all_gather | solution.py:57
  159.2 2.8 reshape.46
  162.0 1.9 copy.84
  163.9 14.4 %all_gather.9 = bf16[256,512]{1,0:T(8,128)(2,1)S(1)} all-gather(bf16[64,512]{1,0:T(8,128)(2,1)S(1)} %bitcast.171), channel_id=1, replica_groups=mesh['doc'=4,'ctx'=8] {'doc'}, dimensions={0}, use_global_device_ids=true | all-gather | bytes 327680 | tf_op jit(solution)/shard_map/all_gather | solution.py:58
  178.6 4.3 %reshape.40 = bf16[4096,1,128]{2,1,0:T(2,128)(2,1)S(1)} reshape(bf16[8,2,32768]{2,1,0:T(2,128)(2,1)} %copy-done.2) | data formatting | bytes 2097152
  183.0 1.2 copy.111
  184.1 1.5 copy.76
  186.1 5.8 %reshape.44 = bf16[4096,1,128]{2,1,0:T(2,128)(2,1)} reshape(bf16[8,2,32768]{2,1,0:T(2,128)(2,1)} %all-to-all-done.2) | data formatting | bytes 2097152
  191.8 1.7 copy.112
  193.5 1.3 copy.82
  194.8 2.2 reshape_reshape_squeeze.7
  197.0 1.4 copy.89
  198.4 2.1 while.27
  200.5 15.9 %while.28 = (s32[]{:T(128)}, f32[256,4,128]{0,2,1:T(8,128)}, f32[256,4,128]{0,2,1:T(8,128)S(1)}, f32[2,512,4,128]{3,2,1,0:T(4,128)}, bf16[2,512,4,128]{3,1,2,0:T...) while((s32[]{:T(128)}, f32[256,4,128]{0,2,1:T(8,128)}, ...), condition=%wide.region_5.6_spmd.clone, body=%wide.region_4.5_spmd.clone.sunk | while | flops 2687369216 | bytes 41730320 | solution.py:89
  200.5 0.8 exponential_divide_fusion.2
  201.3 1.1 fusion.64
  202.4 0.7 subtract_multiply_fusion.2
  203.5 1.2 fusion.63
  204.7 1.1 fusion.65
  205.8 0.7 copy-done.3
  206.4 0.7 copy_dynamic-update-slice_fusion.2
  207.2 1.3 copy-done.4
  208.5 0.7 exponential_divide_fusion.2
  209.3 1.1 fusion.64
  210.4 0.7 subtract_multiply_fusion.2
  211.4 1.2 fusion.63
  212.6 1.1 fusion.65
  213.7 0.7 copy-done.3
  214.4 0.7 copy_dynamic-update-slice_fusion.2
  215.1 1.3 copy-done.4
  216.5 2.0 copy.105
  218.6 1.0 copy.107
  219.6 22.2 %reduce-scatter.7.cloned.1.call-done = f32[64,512]{1,0:T(8,128)} async-done(((f32[256,512]{1,0:T(8,128)}), f32[64,512]{1,0:T(8,128)}) %reduce-scatter.7.cloned.1.call-update) | async-done | bytes 131088
  241.8 1.0 copy.106
  242.8 0.8 copy.98
  243.6 3.5 %all-to-all-start.5 = ((f32[1,64,512]{2,0,1:T(1,128)}), f32[1,64,512]{2,0,1:T(1,128)S(1)}, u32[]{:S(2)}, u32[]{:S(2)}) async-start(f32[1,64,512]{2,0,1:T(1,128)} %copy.98), calls=%async_computation.5 | async-start | bytes 262144 | tf_op jit(solution)/shard_map/all_to_all | solution.py:102
  247.1 16.8 %reduce-scatter.9.cloned.1.call-done = f32[64,512]{1,0:T(8,128)} async-done(((f32[256,512]{1,0:T(8,128)}), f32[64,512]{1,0:T(8,128)}) %reduce-scatter.9.cloned.1.call-update) | async-done | bytes 131088
  263.9 1.0 copy.108
  265.1 8.9 %all_to_all.114 = f32[1,64,512]{2,0,1:T(1,128)S(1)} all-to-all(f32[1,64,512]{2,0,1:T(1,128)S(1)} %copy.100), channel_id=1, replica_groups=mesh['doc'=4,'ctx'=8] {'ctx'}, dimensions={1} | all-to-all | bytes 262144 | tf_op jit(solution)/shard_map/all_to_all | solution.py:103
  274.0 3.6 %all-to-all-start.4 = ((f32[1,1024,512]{2,0,1:T(1,128)}), f32[1,1024,512]{2,0,1:T(1,128)S(1)}, u32[]{:S(2)}, u32[]{:S(2)}) async-start(f32[1,1024,512]{2,0,1:T(1,128)} %bitcast.161), calls=%async_computation.4 | async-start | bytes 4194304 | tf_op jit(solution)/shard_map/all_to_all | solution.py:101
  277.6 0.7 copy.99
  278.3 0.7 copy.101
  278.9 25.2 %all-to-all-done.4 = f32[1,1024,512]{2,0,1:T(1,128)S(1)} async-done(((f32[1,1024,512]{2,0,1:T(1,128)}), f32[1,1024,512]{2,0,1:T(1,128)S(1)}, u32[]{:S(2)}, u32[]{:S(2)}) %all-to-all-start.4) | async-done | bytes 2097184 | tf_op jit(solution)/shard_map/all_to_all | solution.py:101
  304.2 1.5 copy.113
  305.7 1.9 copy.97
  307.6 1.8 copy.102
  (51 shorter events, 4.7 us)
Async XLA Ops:
  11.9 29.2 %copy-start.5 = (bf16[1,8,4096]{2,1,0:T(8,128)(2,1)S(1)}, bf16[1,8,4096]{2,1,0:T(8,128)(2,1)}, u32[]{:S(2)}) copy-start(bf16[1,8,4096]{2,1,0:T(8,128)(2,1)} %param.11) | copy-start | bytes 196612
  36.0 32.0 %all-to-all-start.1 = ((bf16[8,2,2048]{2,1,0:T(2,128)(2,1)}), bf16[8,2,2048]{2,1,0:T(2,128)(2,1)S(1)}, u32[]{:S(2)}, u32[]{:S(2)}) async-start(bf16[8,2,2048]{2,1,0:T(2,128)(2,1)} %reshape.41), calls=%async_computation.1 | async-start | bytes 131072 | tf_op jit(solution)/shard_map/all_to_all | solution.py:35
  68.0 32.6 %all-to-all-start.3 = ((bf16[8,2,2048]{2,1,0:T(2,128)(2,1)}), bf16[8,2,2048]{2,1,0:T(2,128)(2,1)S(1)}, u32[]{:S(2)}, u32[]{:S(2)}) async-start(bf16[8,2,2048]{2,1,0:T(2,128)(2,1)} %reshape.45), calls=%async_computation.3 | async-start | bytes 131072 | tf_op jit(solution)/shard_map/all_to_all | solution.py:36
  100.6 34.7 %all-to-all-start = ((bf16[8,2,32768]{2,1,0:T(2,128)(2,1)}), bf16[8,2,32768]{2,1,0:T(2,128)(2,1)S(1)}, u32[]{:S(2)}, u32[]{:S(2)}) async-start(bf16[8,2,32768]{2,1,0:T(2,128)(2,1)} %reshape.39), calls=%async_computation | async-start | bytes 2097152 | tf_op jit(solution)/shard_map/all_to_all | solution.py:33
  135.3 4.3 %copy-start.2 = (bf16[8,2,32768]{2,1,0:T(2,128)(2,1)}, bf16[8,2,32768]{2,1,0:T(2,128)(2,1)S(1)}, u32[]{:S(2)}) copy-start(bf16[8,2,32768]{2,1,0:T(2,128)(2,1)S(1)} %all-to-all-done) | copy-start | bytes 3145732
  135.3 50.7 %all-to-all-start.2 = ((bf16[8,2,32768]{2,1,0:T(2,128)(2,1)}), bf16[8,2,32768]{2,1,0:T(2,128)(2,1)}, u32[]{:S(2)}, u32[]{:S(2)}) async-start(bf16[8,2,32768]{2,1,0:T(2,128)(2,1)} %reshape.43), calls=%async_computation.2 | async-start | bytes 2097152 | tf_op jit(solution)/shard_map/all_to_all | solution.py:34
  139.6 102.2 %reduce-scatter.7.cloned.1.call-start = ((), (), s32[]{:S(2)}) async-start(), calls=%async_computation.9 | async-start | bytes 655360
  202.4 1.0 copy-start
  204.6 2.5 copy-start.1
  204.6 1.8 copy-start.3
  207.2 1.3 copy-start.4
  210.4 1.0 copy-start
  212.6 2.5 copy-start.1
  212.6 1.8 copy-start.3
  215.1 1.3 copy-start.4
  218.5 45.4 %reduce-scatter.9.cloned.1.call-start = ((), (), s32[]{:S(2)}) async-start(), calls=%async_computation.10 | async-start | bytes 655360
  243.6 21.5 %all-to-all-start.5 = ((f32[1,64,512]{2,0,1:T(1,128)}), f32[1,64,512]{2,0,1:T(1,128)S(1)}, u32[]{:S(2)}, u32[]{:S(2)}) async-start(f32[1,64,512]{2,0,1:T(1,128)} %copy.98), calls=%async_computation.5 | async-start | bytes 262144 | tf_op jit(solution)/shard_map/all_to_all | solution.py:102
  274.0 30.2 %all-to-all-start.4 = ((f32[1,1024,512]{2,0,1:T(1,128)}), f32[1,1024,512]{2,0,1:T(1,128)S(1)}, u32[]{:S(2)}, u32[]{:S(2)}) async-start(f32[1,1024,512]{2,0,1:T(1,128)} %bitcast.161), calls=%async_computation.4 | async-start | bytes 4194304 | tf_op jit(solution)/shard_map/all_to_all | solution.py:101
Sparse Core Ops, SparseCore 0:
  218.6 23.0 reduce-scatter.6
  244.0 19.7 reduce-scatter.8
where the time goes:
time: 318 us; the launch traced here: 316 us
  other arithmetic  90.3 us (28%)
  local copies, waits for them, and re-layouts  72.7 us (23%)
  waiting for transfers between devices  64.3 us (20%)
  blocking collectives  37.8 us (12%)
  starting transfers between devices  25 us (8%)
  between operations  14.4 us (5%)
  matrix products  11.6 us (4%)
    unnamed x6, other arithmetic  90.3 us
    unnamed x29, local copies, waits for them, and re-layouts  51.5 us
    unnamed x4, waiting for transfers between devices  39 us
    all_to_all x1, waiting for transfers between devices, shards(): lax.all_to_all(grad_q[None], 'ctx', split_axis=1, concat_axis=2, tiled=True)  25.2 us
    all_gather x1, blocking collectives, shards(): lax.all_gather(k_heads[0], 'doc', axis=0, tiled=True)  14.5 us
    all_gather x1, blocking collectives, shards(): lax.all_gather(v_heads[0], 'doc', axis=0, tiled=True)  14.4 us
    all_to_all x1, blocking collectives, shards(): lax.all_to_all(grad_v[None], 'ctx', split_axis=1, concat_axis=2, tiled=True)  8.94 us
  transfers between devices with their start and end apart: 8, of which 3 were waited for; matrix products, arithmetic and copies ran while one was open for 34% of the time, Pallas kernels for 0%

commit v1 on v0

v1 whole, which is shorter than its diff:
```python
import functools

import jax
import jax.numpy as jnp
from jax import lax
from jax.experimental import pallas as pl
from jax.experimental.pallas import tpu as pltpu
from jax.sharding import PartitionSpec as P

HD = 128
MESH = pl.DeviceIdType.MESH
NT = (((1,), (1,)), ((), ()))
NN = (((1,), (0,)), ((), ()))
TN = (((0,), (0,)), ((), ()))


def dot(a, b, dims):
    return lax.dot_general(a, b, dims, preferred_element_type=jnp.float32)


def partner(me, step, n):
    if n & (n - 1):
        return lax.rem(me + step, n)
    out, bit = 0, 1
    while bit < n:
        out = out + ((me // bit + step // bit) % 2) * bit
        bit *= 2
    return out


def source(me, step, n):
    if n & (n - 1):
        return lax.rem(me - step + n, n)
    return partner(me, step, n)


def split16(x):
    high = x.astype(jnp.bfloat16)
    return high, (x - high.astype(jnp.float32)).astype(jnp.bfloat16)


def kernel(
    n, ndoc, rows, rows_p,
    q_ref, g_ref, kv_ref,
    gq_out, gk_out, gv_out,
    qbuf, gbuf, kvbuf, keys, values, gqbuf, acc, rsbuf, fin_src, fin,
    kvs, kvr, qs, qr, gs, gr, zs, zr, os, orr, rs, rr, fs, fr,
):
    c = lax.axis_index("ctx")
    d = lax.axis_index("doc")
    width = qbuf.shape[2]
    nheads = width // HD
    total = ndoc * n * rows_p

    def cols(i):
        return pl.ds(pl.multiple_of(i * width, width), width)

    barrier = pltpu.get_barrier_semaphore()

    @pl.loop(1, n)
    def _(s):
        pl.semaphore_signal(barrier, inc=1, device_id=(d, lax.rem(c + s, n)), device_id_type=MESH)

    @pl.loop(1, ndoc)
    def _(t):
        pl.semaphore_signal(barrier, inc=1, device_id=(lax.rem(d + t, ndoc), c), device_id_type=MESH)

    pl.semaphore_wait(barrier, n - 1 + ndoc - 1)

    def kv_send(p):
        return pltpu.make_async_remote_copy(
            src_ref=kv_ref.at[:, cols(p)], dst_ref=kvbuf.at[d * n + c],
            send_sem=kvs.at[p], recv_sem=kvr.at[c], device_id=(d, p), device_id_type=MESH)

    def q_send(p):
        return pltpu.make_async_remote_copy(
            src_ref=q_ref.at[:, cols(p)], dst_ref=qbuf.at[c],
            send_sem=qs.at[p], recv_sem=qr.at[c], device_id=(d, p), device_id_type=MESH)

    def g_send(p):
        return pltpu.make_async_remote_copy(
            src_ref=g_ref.at[:, cols(p)], dst_ref=gbuf.at[c],
            send_sem=gs.at[p], recv_sem=gr.at[c], device_id=(d, p), device_id_type=MESH)

    def z_send(t):
        return pltpu.make_async_remote_copy(
            src_ref=kvbuf.at[pl.ds(d * n, n)], dst_ref=kvbuf.at[pl.ds(d * n, n)],
            send_sem=zs.at[t], recv_sem=zr.at[t],
            device_id=(lax.rem(d + t, ndoc), c), device_id_type=MESH)

    def o_send(p):
        return pltpu.make_async_remote_copy(
            src_ref=gqbuf.at[p], dst_ref=gq_out.at[:, cols(c)],
            send_sem=os.at[p], recv_sem=orr.at[c], device_id=(d, p), device_id_type=MESH)

    def r_send(t):
        to = lax.rem(d + t, ndoc)
        return pltpu.make_async_remote_copy(
            src_ref=acc.at[pl.ds(to * n, n)], dst_ref=rsbuf.at[t],
            send_sem=rs.at[t], recv_sem=rr.at[t], device_id=(to, c), device_id_type=MESH)

    def f_send(p):
        return pltpu.make_async_remote_copy(
            src_ref=fin_src.at[p], dst_ref=fin.at[c],
            send_sem=fs.at[p], recv_sem=fr.at[c], device_id=(d, p), device_id_type=MESH)

    kv_own = pltpu.make_async_copy(kv_ref.at[:, cols(c)], kvbuf.at[d * n + c], kvr.at[c])
    q_own = pltpu.make_async_copy(q_ref.at[:, cols(c)], qbuf.at[c], qr.at[c])
    g_own = pltpu.make_async_copy(g_ref.at[:, cols(c)], gbuf.at[c], gr.at[c])
    kv_own.start()

    @pl.loop(1, n)
    def _(s):
        kv_send(partner(c, s, n)).start()

    q_own.start()
    g_own.start()

    @pl.loop(1, n)
    def _(s):
        p = partner(c, s, n)
        q_send(p).start()
        g_send(p).start()

    @pl.loop(0, n)
    def _(i):
        slab = kvbuf.at[d * n + i]
        pltpu.make_async_copy(slab, slab, kvr.at[i]).wait()

    @pl.loop(1, ndoc)
    def _(t):
        z_send(t).start()

    acc[...] = jnp.zeros_like(acc)

    @pl.loop(1, ndoc)
    def _(t):
        slab = kvbuf.at[pl.ds(lax.rem(d - t + ndoc, ndoc) * n, n)]
        pltpu.make_async_copy(slab, slab, zr.at[t]).wait()

    both = kvbuf[...].astype(jnp.float32)
    keys[...] = both[:, :rows_p].reshape(total, width).astype(jnp.bfloat16)
    values[...] = both[:, rows_p:].reshape(total, width).astype(jnp.bfloat16)

    scale = HD ** (-0.5)

    def step(s, carry):
        p = source(c, s, n)
        pltpu.make_async_copy(qbuf.at[p], qbuf.at[p], qr.at[p]).wait()
        pltpu.make_async_copy(gbuf.at[p], gbuf.at[p], gr.at[p]).wait()
        for h in range(nheads):
            at = slice(h * HD, (h + 1) * HD)
            q, g = qbuf[p, :, at], gbuf[p, :, at]
            k, v = keys[:, at], values[:, at]
            expo = jnp.exp(dot(k, q, NT) * scale)
            if rows_p != rows:
                place = lax.broadcasted_iota(jnp.int32, expo.shape, 0)
                expo = jnp.where(lax.rem(place, rows_p) < rows, expo, 0.0)
            dprob = dot(v, g, NT)
            norm = jnp.sum(expo, axis=0, keepdims=True)
            drift = jnp.sum(expo * dprob, axis=0, keepdims=True) / norm
            prob = expo * (1.0 / norm)
            dscore = prob * (dprob - drift) * scale
            ds_hi, ds_lo = split16(dscore)
            pr_hi, pr_lo = split16(prob)
            gqbuf[p, :, at] = dot(ds_hi, k, TN) + dot(ds_lo, k, TN)
            grad_k = dot(ds_hi, q, NN) + dot(ds_lo, q, NN)
            grad_v = dot(pr_hi, g, NN) + dot(pr_lo, g, NN)
            acc[:, :rows_p, at] += grad_k.reshape(ndoc * n, rows_p, HD)
            acc[:, rows_p:, at] += grad_v.reshape(ndoc * n, rows_p, HD)

        @pl.when(s > 0)
        def _():
            o_send(p).start()

        return carry

    lax.fori_loop(0, n, step, 0)

    @pl.loop(1, ndoc)
    def _(t):
        r_send(t).start()

    gq_own = pltpu.make_async_copy(gqbuf.at[c], gq_out.at[:, cols(c)], orr.at[c])
    gq_own.start()
    fin_src[...] = acc[pl.ds(d * n, n)]

    @pl.loop(1, ndoc)
    def _(t):
        r_send(t).wait_recv()
        fin_src[...] += rsbuf[t]

    @pl.loop(1, n)
    def _(s):
        f_send(partner(c, s, n)).start()

    fin[c] = fin_src[c]

    @pl.loop(1, n)
    def _(s):
        p = source(c, s, n)
        pltpu.make_async_copy(fin.at[p], fin.at[p], fr.at[p]).wait()

    for i in range(n):
        at = slice(i * width, (i + 1) * width)
        gk_out[:, at] = fin[i, :rows]
        gv_out[:, at] = fin[i, rows_p:rows_p + rows]

    @pl.loop(0, n)
    def _(i):
        mine = gq_out.at[:, cols(i)]
        pltpu.make_async_copy(mine, mine, orr.at[i]).wait()

    @pl.loop(1, n)
    def _(s):
        p = partner(c, s, n)
        kv_send(p).wait_send()
        q_send(p).wait_send()
        g_send(p).wait_send()
        o_send(p).wait_send()
        f_send(p).wait_send()

    @pl.loop(1, ndoc)
    def _(t):
        z_send(t).wait_send()
        r_send(t).wait_send()


def shards(queries, out_grad, mem_keys, mem_values):
    n, ndoc = lax.axis_size("ctx"), lax.axis_size("doc")
    qrows, features = queries.shape[1:]
    rows = mem_keys.shape[1]
    rows_p = -(-rows // 8) * 8
    width = features // n
    slabs = ndoc * n
    pad = ((0, rows_p - rows), (0, 0))
    kv = jnp.concatenate([jnp.pad(mem_keys[0], pad), jnp.pad(mem_values[0], pad)], axis=0)
    dma = pltpu.SemaphoreType.DMA
    vmem = pl.BlockSpec(memory_space=pltpu.VMEM)
    hbm = pl.BlockSpec(memory_space=pl.ANY)
    pairs = slabs * rows_p * n * qrows * width
    gq, gk, gv = pl.pallas_call(
        functools.partial(kernel, n, ndoc, rows, rows_p),
        out_shape=(
            jax.ShapeDtypeStruct((qrows, features), jnp.float32),
            jax.ShapeDtypeStruct((rows, features), jnp.float32),
            jax.ShapeDtypeStruct((rows, features), jnp.float32),
        ),
        in_specs=[hbm, hbm, hbm],
        out_specs=(hbm, vmem, vmem),
        scratch_shapes=[
            pltpu.VMEM((n, qrows, width), jnp.bfloat16),
            pltpu.VMEM((n, qrows, width), jnp.bfloat16),
            pltpu.VMEM((slabs, 2 * rows_p, width), jnp.bfloat16),
            pltpu.VMEM((slabs * rows_p, width), jnp.bfloat16),
            pltpu.VMEM((slabs * rows_p, width), jnp.bfloat16),
            pltpu.VMEM((n, qrows, width), jnp.float32),
            pltpu.VMEM((slabs, 2 * rows_p, width), jnp.float32),
            pltpu.VMEM((ndoc, n, 2 * rows_p, width), jnp.float32),
            pltpu.VMEM((n, 2 * rows_p, width), jnp.float32),
            pltpu.VMEM((n, 2 * rows_p, width), jnp.float32),
            dma((n,)), dma((n,)), dma((n,)), dma((n,)), dma((n,)), dma((n,)),
            dma((ndoc,)), dma((ndoc,)), dma((n,)), dma((n,)),
            dma((ndoc,)), dma((ndoc,)), dma((n,)), dma((n,)),
        ],
        compiler_params=pltpu.CompilerParams(
            collective_id=0, has_side_effects=True, vmem_limit_bytes=48 * 1024 * 1024),
        cost_estimate=pl.CostEstimate(
            flops=16 * pairs, bytes_accessed=8 * qrows * features, transcendentals=pairs // HD),
    )(queries[0], out_grad[0], kv)
    return gq[None], gk[None], gv[None]


def solution(mesh):
    placed = P("doc", "ctx", None)
    return jax.shard_map(
        shards,
        mesh=mesh,
        in_specs=(placed,) * 4,
        out_specs=(placed,) * 3,
        check_vma=False,
    )
```

time: 318 us -> 69.8 us (0.22)
  the two profiles are of different devices: /device:TPU:0 before, /device:TPU:25 now
where the time goes in v1:
time: 69.8 us; the launch traced here: 69.5 us
  Pallas kernels  62.9 us (90%)
  local copies, waits for them, and re-layouts  5.08 us (7%)
  other arithmetic  0.88 us (1%)
    pallas_call x1, Pallas kernels, shards(): pl.pallas_call(functools.partial(kernel, n, ndoc, rows, rows_p), out_shap...  62.9 us
    unnamed x7, local copies, waits for them, and re-layouts  5.08 us

profile of v1, /device:TPU:25, one launch (start us, length us, event | category | flops | bytes accessed | tf_op | source)
XLA Modules:
  0.0 69.5 jit_solution(18000783814115226251)
XLA Ops:
  0.6 0.9 %pad_maximum_fusion.kv_ref = bf16[16,4096]{1,0:T(8,128)(2,1)S(1)} fusion(bf16[8,4096]{1,0:T(8,128)(2,1)} %bitcast.12, bf16[8,4096]{1,0:T(8,128)(2,1)} %bitcast.13), kind=kLoop, calls=%fused_computation | loop fusion | flops 262144 | bytes 262144 | tf_op jit(solution)/shard_map/concatenate | solution.py:237
  1.5 0.0 copy-start
  1.5 1.2 %copy-done = bf16[1,128,4096]{2,1,0:T(8,128)(2,1)S(1)} copy-done((bf16[1,128,4096]{2,1,0:T(8,128)(2,1)S(1)}, bf16[1,128,4096]{2,1,0:T(8,128)(2,1)}, u32[]{:S(2)}) %copy-start) | copy-done | bytes 1048600
  2.7 0.0 copy-start.1
  2.7 1.2 %copy-done.1 = bf16[1,128,4096]{2,1,0:T(8,128)(2,1)S(1)} copy-done((bf16[1,128,4096]{2,1,0:T(8,128)(2,1)S(1)}, bf16[1,128,4096]{2,1,0:T(8,128)(2,1)}, u32[]{:S(2)}) %copy-start.1) | copy-done | bytes 1048600
  4.0 62.9 %shard_map.67 = (f32[128,4096]{1,0:T(8,128)S(1)}, f32[8,4096]{1,0:T(8,128)S(1)}, f32[8,4096]{1,0:T(8,128)S(1)}) custom-call(bf16[128,4096]{1,0:T(8,128)(2,1)S(1)} %bitcast.10, bf16[128,4096]{1,0:T(8,128)(2,1)S(1)} %bitcast.11, bf16[16,4096]{1,0:T(8,128)(2,1)S(1)} %pad_maximum_fusion.kv_ref), custom_call_target="tpu_custom_call" | custom-call | flops 2147483648 | bytes 4194304 | tf_op jit(solution)/shard_map/pallas_call | solution.py:242
  66.9 1.3 %copy.10 = f32[1,128,4096]{2,1,0:T(8,128)} copy(f32[1,128,4096]{2,1,0:T(8,128)S(1)} %bitcast.7) | data formatting | bytes 4194304
  68.2 0.7 copy.11
  68.9 0.7 copy.12
Async XLA Ops:
  1.5 1.2 %copy-start = (bf16[1,128,4096]{2,1,0:T(8,128)(2,1)S(1)}, bf16[1,128,4096]{2,1,0:T(8,128)(2,1)}, u32[]{:S(2)}) copy-start(bf16[1,128,4096]{2,1,0:T(8,128)(2,1)} %param.4) | copy-start | bytes 3145732
  2.7 1.2 %copy-start.1 = (bf16[1,128,4096]{2,1,0:T(8,128)(2,1)S(1)}, bf16[1,128,4096]{2,1,0:T(8,128)(2,1)}, u32[]{:S(2)}) copy-start(bf16[1,128,4096]{2,1,0:T(8,128)(2,1)} %param.5) | copy-start | bytes 3145732

commit v2 on v1

--- a/solution.py
+++ b/solution.py
@@ -34,6 +34,28 @@
     return partner(me, step, n)
 
 
+TOP = 2.0 ** 15.5
+
+
+def peak_of(x, axis):
+    return jnp.maximum(jnp.max(jnp.abs(x), axis=axis, keepdims=True), 1e-30)
+
+
+def encode(x, peak):
+    y = x * (TOP / peak)
+    y = y * y
+    y = y * y
+    y = y * y
+    return jnp.where(x < 0, -y, y).astype(jnp.bfloat16)
+
+
+def decode(y, peak):
+    y = y.astype(jnp.float32)
+    fourth = lax.rsqrt(lax.rsqrt(jnp.maximum(jnp.abs(y), 1e-37)))
+    x = fourth * lax.rsqrt(fourth) * (peak * (1.0 / TOP))
+    return jnp.where(y < 0, -x, x)
+
+
 def split16(x):
     high = x.astype(jnp.bfloat16)
     return high, (x - high.astype(jnp.float32)).astype(jnp.bfloat16)
@@ -42,9 +64,9 @@
 def kernel(
     n, ndoc, rows, rows_p,
     q_ref, g_ref, kv_ref,
-    gq_out, gk_out, gv_out,
-    qbuf, gbuf, kvbuf, keys, values, gqbuf, acc, rsbuf, fin_src, fin,
-    kvs, kvr, qs, qr, gs, gr, zs, zr, os, orr, rs, rr, fs, fr,
+    gq_out, gqp_out, gkv_out,
+    qbuf, gbuf, kvbuf, keys, values, gqbuf, gqp, acc, part, partp, rsbuf, rspbuf, fin_src, fin,
+    kvs, kvr, qs, qr, gs, gr, zs, zr, os, orr, ps, pr, rs, rr, ts, tr, fs, fr,
 ):
     c = lax.axis_index("ctx")
     d = lax.axis_index("doc")
@@ -93,11 +115,22 @@
             src_ref=gqbuf.at[p], dst_ref=gq_out.at[:, cols(c)],
             send_sem=os.at[p], recv_sem=orr.at[c], device_id=(d, p), device_id_type=MESH)
 
+    def p_send(p):
+        return pltpu.make_async_remote_copy(
+            src_ref=gqp.at[p], dst_ref=gqp_out.at[:, cols(c)],
+            send_sem=ps.at[p], recv_sem=pr.at[c], device_id=(d, p), device_id_type=MESH)
+
     def r_send(t):
         to = lax.rem(d + t, ndoc)
         return pltpu.make_async_remote_copy(
-            src_ref=acc.at[pl.ds(to * n, n)], dst_ref=rsbuf.at[t],
+            src_ref=part.at[pl.ds(to * n, n)], dst_ref=rsbuf.at[t],
             send_sem=rs.at[t], recv_sem=rr.at[t], device_id=(to, c), device_id_type=MESH)
+
+    def t_send(t):
+        return pltpu.make_async_remote_copy(
+            src_ref=partp, dst_ref=rspbuf.at[t],
+            send_sem=ts.at[t], recv_sem=tr.at[t],
+            device_id=(lax.rem(d + t, ndoc), c), device_id_type=MESH)
 
     def f_send(p):
         return pltpu.make_async_remote_copy(
@@ -163,7 +196,10 @@
             dscore = prob * (dprob - drift) * scale
             ds_hi, ds_lo = split16(dscore)
             pr_hi, pr_lo = split16(prob)
-            gqbuf[p, :, at] = dot(ds_hi, k, TN) + dot(ds_lo, k, TN)
+            grad_q = dot(ds_hi, k, TN) + dot(ds_lo, k, TN)
+            peak = peak_of(grad_q, 0)
+            gqp[p, :, at] = jnp.broadcast_to(peak, (8, HD))
+            gqbuf[p, :, at] = encode(grad_q, peak)
             grad_k = dot(ds_hi, q, NN) + dot(ds_lo, q, NN)
             grad_v = dot(pr_hi, g, NN) + dot(pr_lo, g, NN)
             acc[:, :rows_p, at] += grad_k.reshape(ndoc * n, rows_p, HD)
@@ -172,23 +208,37 @@
         @pl.when(s > 0)
         def _():
             o_send(p).start()
+            p_send(p).start()
 
         return carry
 
     lax.fori_loop(0, n, step, 0)
 
-    @pl.loop(1, ndoc)
-    def _(t):
+    peak_k = peak_of(acc[:, :rows_p].reshape(total, width), 0)
+    peak_v = peak_of(acc[:, rows_p:].reshape(total, width), 0)
+    partp[...] = jnp.where(lax.broadcasted_iota(jnp.int32, (8, width), 0) < 4, peak_k, peak_v)
+    lower = lax.broadcasted_iota(jnp.int32, (2 * rows_p, width), 0) < rows_p
+    peaks = jnp.where(lower, peak_k, peak_v)
+
+    @pl.loop(1, ndoc)
+    def _(t):
+        to = pl.ds(lax.rem(d + t, ndoc) * n, n)
+        part[to] = encode(acc[to], peaks[None])
+        t_send(t).start()
         r_send(t).start()
 
     gq_own = pltpu.make_async_copy(gqbuf.at[c], gq_out.at[:, cols(c)], orr.at[c])
     gq_own.start()
+    gqp_own = pltpu.make_async_copy(gqp.at[c], gqp_out.at[:, cols(c)], pr.at[c])
+    gqp_own.start()
     fin_src[...] = acc[pl.ds(d * n, n)]
 
     @pl.loop(1, ndoc)
     def _(t):
+        t_send(t).wait_recv()
         r_send(t).wait_recv()
-        fin_src[...] += rsbuf[t]
+        far = jnp.where(lower, rspbuf[t, 0:1], rspbuf[t, 4:5])
+        fin_src[...] += decode(rsbuf[t], far[None])
 
     @pl.loop(1, n)
     def _(s):
@@ -203,13 +253,14 @@
 
     for i in range(n):
         at = slice(i * width, (i + 1) * width)
-        gk_out[:, at] = fin[i, :rows]
-        gv_out[:, at] = fin[i, rows_p:rows_p + rows]
+        gkv_out[:, at] = fin[i]
 
     @pl.loop(0, n)
     def _(i):
         mine = gq_out.at[:, cols(i)]
         pltpu.make_async_copy(mine, mine, orr.at[i]).wait()
+        peaks_in = gqp_out.at[:, cols(i)]
+        pltpu.make_async_copy(peaks_in, peaks_in, pr.at[i]).wait()
 
     @pl.loop(1, n)
     def _(s):
@@ -218,12 +269,14 @@
         q_send(p).wait_send()
         g_send(p).wait_send()
         o_send(p).wait_send()
+        p_send(p).wait_send()
         f_send(p).wait_send()
 
     @pl.loop(1, ndoc)
     def _(t):
         z_send(t).wait_send()
         r_send(t).wait_send()
+        t_send(t).wait_send()
 
 
 def shards(queries, out_grad, mem_keys, mem_values):
@@ -239,36 +292,41 @@
     vmem = pl.BlockSpec(memory_space=pltpu.VMEM)
     hbm = pl.BlockSpec(memory_space=pl.ANY)
     pairs = slabs * rows_p * n * qrows * width
-    gq, gk, gv = pl.pallas_call(
+    gq, gqp, gkv = pl.pallas_call(
         functools.partial(kernel, n, ndoc, rows, rows_p),
         out_shape=(
-            jax.ShapeDtypeStruct((qrows, features), jnp.float32),
-            jax.ShapeDtypeStruct((rows, features), jnp.float32),
-            jax.ShapeDtypeStruct((rows, features), jnp.float32),
+            jax.ShapeDtypeStruct((qrows, features), jnp.bfloat16),
+            jax.ShapeDtypeStruct((8, features), jnp.float32),
+            jax.ShapeDtypeStruct((2 * rows_p, features), jnp.float32),
         ),
         in_specs=[hbm, hbm, hbm],
-        out_specs=(hbm, vmem, vmem),
+        out_specs=(vmem, vmem, vmem),
         scratch_shapes=[
             pltpu.VMEM((n, qrows, width), jnp.bfloat16),
             pltpu.VMEM((n, qrows, width), jnp.bfloat16),
             pltpu.VMEM((slabs, 2 * rows_p, width), jnp.bfloat16),
             pltpu.VMEM((slabs * rows_p, width), jnp.bfloat16),
             pltpu.VMEM((slabs * rows_p, width), jnp.bfloat16),
-            pltpu.VMEM((n, qrows, width), jnp.float32),
+            pltpu.VMEM((n, qrows, width), jnp.bfloat16),
+            pltpu.VMEM((n, 8, width), jnp.float32),
             pltpu.VMEM((slabs, 2 * rows_p, width), jnp.float32),
-            pltpu.VMEM((ndoc, n, 2 * rows_p, width), jnp.float32),
+            pltpu.VMEM((slabs, 2 * rows_p, width), jnp.bfloat16),
+            pltpu.VMEM((8, width), jnp.float32),
+            pltpu.VMEM((ndoc, n, 2 * rows_p, width), jnp.bfloat16),
+            pltpu.VMEM((ndoc, 8, width), jnp.float32),
             pltpu.VMEM((n, 2 * rows_p, width), jnp.float32),
             pltpu.VMEM((n, 2 * rows_p, width), jnp.float32),
             dma((n,)), dma((n,)), dma((n,)), dma((n,)), dma((n,)), dma((n,)),
-            dma((ndoc,)), dma((ndoc,)), dma((n,)), dma((n,)),
-            dma((ndoc,)), dma((ndoc,)), dma((n,)), dma((n,)),
+            dma((ndoc,)), dma((ndoc,)), dma((n,)), dma((n,)), dma((n,)), dma((n,)),
+            dma((ndoc,)), dma((ndoc,)), dma((ndoc,)), dma((ndoc,)), dma((n,)), dma((n,)),
         ],
         compiler_params=pltpu.CompilerParams(
-            collective_id=0, has_side_effects=True, vmem_limit_bytes=48 * 1024 * 1024),
+            collective_id=0, has_side_effects=True, vmem_limit_bytes=58 * 1024 * 1024),
         cost_estimate=pl.CostEstimate(
             flops=16 * pairs, bytes_accessed=8 * qrows * features, transcendentals=pairs // HD),
     )(queries[0], out_grad[0], kv)
-    return gq[None], gk[None], gv[None]
+    gq = decode(gq, gqp[0:1])
+    return gq[None], gkv[None, :rows], gkv[None, rows_p:rows_p + rows]
 
 
 def solution(mesh):

time: 69.8 us -> 63.9 us (0.915)
  Pallas kernels: 62.9 us -> 55.5 us
  other arithmetic: 0.88 us -> 5.83 us
  local copies, waits for them, and re-layouts: 5.08 us -> 1.69 us
    pallas_call x1, Pallas kernels: 62.9 us -> 55.5 us  [shards(): pl.pallas_call(functools.partial(kernel, n, ndoc, rows, rows_p), out_shap...]
    unnamed x7 -> x0, local copies, waits for them, and re-layouts: 5.08 us -> none
    broadcast_in_dim x0 -> x1, other arithmetic: none -> 3.37 us  [shards(): return (gq[None], gkv[None, :rows], gkv[None, rows_p:rows_p + rows])]
    broadcast_in_dim x0 -> x1, local copies, waits for them, and re-layouts: none -> 1.69 us  [shards(): return (gq[None], gkv[None, :rows], gkv[None, rows_p:rows_p + rows])]
    mul x0 -> x1, other arithmetic: none -> 0.92 us  [decode(): x = fourth * lax.rsqrt(fourth) * (peak * (1.0 / TOP))]
where the time goes in v2:
time: 63.9 us; the launch traced here: 63.6 us
  Pallas kernels  55.5 us (87%)
  other arithmetic  5.83 us (9%)
  local copies, waits for them, and re-layouts  1.69 us (3%)
  between operations  0.64 us (1%)
    pallas_call x1, Pallas kernels, shards(): pl.pallas_call(functools.partial(kernel, n, ndoc, rows, rows_p), out_shap...  55.5 us
    broadcast_in_dim x1, other arithmetic, shards(): return (gq[None], gkv[None, :rows], gkv[None, rows_p:rows_p + rows])  3.37 us
    broadcast_in_dim x1, local copies, waits for them, and re-layouts, shards(): return (gq[None], gkv[None, :rows], gkv[None, rows_p:rows_p + rows])  1.69 us
    concatenate x1, other arithmetic, shards(): jnp.concatenate([jnp.pad(mem_keys[0], pad), jnp.pad(mem_values[0], pad)],...  1.54 us

profile of v2, /device:TPU:25, one launch (start us, length us, event | category | flops | bytes accessed | tf_op | source)
XLA Modules:
  0.0 63.6 jit_solution(17095743119852977047)
XLA Ops:
  0.6 1.5 %pad_maximum_fusion.kv_ref = bf16[16,4096]{1,0:T(8,128)(2,1)} fusion(bf16[8,4096]{1,0:T(8,128)(2,1)} %bitcast.12, bf16[8,4096]{1,0:T(8,128)(2,1)} %bitcast.13), kind=kLoop, calls=%fused_computation.9 | loop fusion | flops 262144 | bytes 262144 | tf_op jit(solution)/shard_map/concatenate | solution.py:290
  2.2 55.5 %shard_map.67 = (bf16[128,4096]{1,0:T(8,128)(2,1)}, f32[8,4096]{1,0:T(8,128)}, f32[16,4096]{1,0:T(8,128)}) custom-call(bf16[128,4096]{1,0:T(8,128)(2,1)} %bitcast.14, bf16[128,4096]{1,0:T(8,128)(2,1)} %bitcast.15, bf16[16,4096]{1,0:T(8,128)(2,1)} %pad_maximum_fusion.kv_ref), custom_call_target="tpu_custom_call" | custom-call | flops 2147483648 | bytes 4194304 | tf_op jit(solution)/shard_map/pallas_call | solution.py:295
  57.7 0.9 %slice_multiply_fusion = f32[1,4096]{1,0:T(1,128)S(1)} fusion(f32[8,4096]{1,0:T(8,128)} %get-tuple-element.7), kind=kLoop, calls=%fused_computation.12 | loop fusion | flops 4096 | bytes 32768 | tf_op jit(solution)/shard_map/mul | solution.py:55
  58.6 1.7 %slice_bitcast_fusion = (f32[1,8,4096]{2,1,0:T(8,128)}, f32[1,8,4096]{2,1,0:T(8,128)}) fusion(f32[16,4096]{1,0:T(8,128)} %get-tuple-element.8), kind=kLoop, calls=%fused_computation.10 | loop fusion | bytes 524288 | tf_op jit(solution)/shard_map/broadcast_in_dim | solution.py:329
  60.3 3.4 %fusion.4 = f32[1,128,4096]{2,1,0:T(8,128)} fusion(bf16[128,4096]{1,0:T(8,128)(2,1)} %get-tuple-element.6, f32[4096]{0:T(1024)S(1)} %bitcast.11), kind=kLoop, calls=%fused_computation.8 | loop fusion | flops 4194304 | bytes 3162112 | tf_op jit(solution)/shard_map/broadcast_in_dim | solution.py:329

commit v3 on v2

--- a/solution.py
+++ b/solution.py
@@ -65,8 +65,8 @@
     n, ndoc, rows, rows_p,
     q_ref, g_ref, kv_ref,
     gq_out, gqp_out, gkv_out,
-    qbuf, gbuf, kvbuf, keys, values, gqbuf, gqp, acc, part, partp, rsbuf, rspbuf, fin_src, fin,
-    kvs, kvr, qs, qr, gs, gr, zs, zr, os, orr, ps, pr, rs, rr, ts, tr, fs, fr,
+    qbuf, gbuf, kvbuf, keys, values, gqbuf, gqp, acc, part, partp, rsbuf, rspbuf, fin_src, fin_enc, finp, fin, fin_peaks,
+    kvs, kvr, qs, qr, gs, gr, zs, zr, os, orr, ps, pr, rs, rr, ts, tr, fs, fr, us, ur,
 ):
     c = lax.axis_index("ctx")
     d = lax.axis_index("doc")
@@ -117,7 +117,7 @@
 
     def p_send(p):
         return pltpu.make_async_remote_copy(
-            src_ref=gqp.at[p], dst_ref=gqp_out.at[:, cols(c)],
+            src_ref=gqp.at[p], dst_ref=gqp_out.at[c],
             send_sem=ps.at[p], recv_sem=pr.at[c], device_id=(d, p), device_id_type=MESH)
 
     def r_send(t):
@@ -134,8 +134,25 @@
 
     def f_send(p):
         return pltpu.make_async_remote_copy(
-            src_ref=fin_src.at[p], dst_ref=fin.at[c],
+            src_ref=fin_enc.at[p], dst_ref=fin.at[c],
             send_sem=fs.at[p], recv_sem=fr.at[c], device_id=(d, p), device_id_type=MESH)
+
+    def u_send(p):
+        return pltpu.make_async_remote_copy(
+            src_ref=finp, dst_ref=fin_peaks.at[c],
+            send_sem=us.at[p], recv_sem=ur.at[c], device_id=(d, p), device_id_type=MESH)
+
+    lower = lax.broadcasted_iota(jnp.int32, (2 * rows_p, HD), 0) < rows_p
+
+    def note_peaks(tile, x):
+        for first, half in ((0, x[:, :rows_p]), (nheads, x[:, rows_p:])):
+            peak = peak_of(half.reshape(-1, width), 0)
+            for h in range(nheads):
+                tile[first + h:first + h + 1] = peak[:, h * HD:(h + 1) * HD]
+
+    def spread(tile):
+        return jnp.concatenate(
+            [jnp.where(lower, tile[h:h + 1], tile[nheads + h:nheads + h + 1]) for h in range(nheads)], axis=1)
 
     kv_own = pltpu.make_async_copy(kv_ref.at[:, cols(c)], kvbuf.at[d * n + c], kvr.at[c])
     q_own = pltpu.make_async_copy(q_ref.at[:, cols(c)], qbuf.at[c], qr.at[c])
@@ -165,6 +182,9 @@
         z_send(t).start()
 
     acc[...] = jnp.zeros_like(acc)
+    gqp[...] = jnp.zeros_like(gqp)
+    partp[...] = jnp.zeros_like(partp)
+    finp[...] = jnp.zeros_like(finp)
 
     @pl.loop(1, ndoc)
     def _(t):
@@ -198,7 +218,7 @@
             pr_hi, pr_lo = split16(prob)
             grad_q = dot(ds_hi, k, TN) + dot(ds_lo, k, TN)
             peak = peak_of(grad_q, 0)
-            gqp[p, :, at] = jnp.broadcast_to(peak, (8, HD))
+            gqp[p, h:h + 1] = peak
             gqbuf[p, :, at] = encode(grad_q, peak)
             grad_k = dot(ds_hi, q, NN) + dot(ds_lo, q, NN)
             grad_v = dot(pr_hi, g, NN) + dot(pr_lo, g, NN)
@@ -214,11 +234,8 @@
 
     lax.fori_loop(0, n, step, 0)
 
-    peak_k = peak_of(acc[:, :rows_p].reshape(total, width), 0)
-    peak_v = peak_of(acc[:, rows_p:].reshape(total, width), 0)
-    partp[...] = jnp.where(lax.broadcasted_iota(jnp.int32, (8, width), 0) < 4, peak_k, peak_v)
-    lower = lax.broadcasted_iota(jnp.int32, (2 * rows_p, width), 0) < rows_p
-    peaks = jnp.where(lower, peak_k, peak_v)
+    note_peaks(partp, acc[...])
+    peaks = spread(partp[...])
 
     @pl.loop(1, ndoc)
     def _(t):
@@ -229,7 +246,7 @@
 
     gq_own = pltpu.make_async_copy(gqbuf.at[c], gq_out.at[:, cols(c)], orr.at[c])
     gq_own.start()
-    gqp_own = pltpu.make_async_copy(gqp.at[c], gqp_out.at[:, cols(c)], pr.at[c])
+    gqp_own = pltpu.make_async_copy(gqp.at[c], gqp_out.at[c], pr.at[c])
     gqp_own.start()
     fin_src[...] = acc[pl.ds(d * n, n)]
 
@@ -237,29 +254,35 @@
     def _(t):
         t_send(t).wait_recv()
         r_send(t).wait_recv()
-        far = jnp.where(lower, rspbuf[t, 0:1], rspbuf[t, 4:5])
-        fin_src[...] += decode(rsbuf[t], far[None])
-
-    @pl.loop(1, n)
-    def _(s):
-        f_send(partner(c, s, n)).start()
-
-    fin[c] = fin_src[c]
+        fin_src[...] += decode(rsbuf[t], spread(rspbuf[t])[None])
+
+    note_peaks(finp, fin_src[...])
+    fin_enc[...] = encode(fin_src[...], spread(finp[...])[None])
+
+    @pl.loop(1, n)
+    def _(s):
+        p = partner(c, s, n)
+        u_send(p).start()
+        f_send(p).start()
+
+    fin[c] = fin_enc[c]
+    fin_peaks[c] = finp[...]
 
     @pl.loop(1, n)
     def _(s):
         p = source(c, s, n)
         pltpu.make_async_copy(fin.at[p], fin.at[p], fr.at[p]).wait()
+        pltpu.make_async_copy(fin_peaks.at[p], fin_peaks.at[p], ur.at[p]).wait()
 
     for i in range(n):
         at = slice(i * width, (i + 1) * width)
-        gkv_out[:, at] = fin[i]
+        gkv_out[:, at] = decode(fin[i], spread(fin_peaks[i]))
 
     @pl.loop(0, n)
     def _(i):
         mine = gq_out.at[:, cols(i)]
         pltpu.make_async_copy(mine, mine, orr.at[i]).wait()
-        peaks_in = gqp_out.at[:, cols(i)]
+        peaks_in = gqp_out.at[i]
         pltpu.make_async_copy(peaks_in, peaks_in, pr.at[i]).wait()
 
     @pl.loop(1, n)
@@ -271,20 +294,26 @@
         o_send(p).wait_send()
         p_send(p).wait_send()
         f_send(p).wait_send()
+        u_send(p).wait_send()
 
     @pl.loop(1, ndoc)
     def _(t):
         z_send(t).wait_send()
         r_send(t).wait_send()
         t_send(t).wait_send()
+
+
+def up8(x):
+    return -(-x // 8) * 8
 
 
 def shards(queries, out_grad, mem_keys, mem_values):
     n, ndoc = lax.axis_size("ctx"), lax.axis_size("doc")
     qrows, features = queries.shape[1:]
     rows = mem_keys.shape[1]
-    rows_p = -(-rows // 8) * 8
+    rows_p = up8(rows)
     width = features // n
+    nheads = width // HD
     slabs = ndoc * n
     pad = ((0, rows_p - rows), (0, 0))
     kv = jnp.concatenate([jnp.pad(mem_keys[0], pad), jnp.pad(mem_values[0], pad)], axis=0)
@@ -296,7 +325,7 @@
         functools.partial(kernel, n, ndoc, rows, rows_p),
         out_shape=(
             jax.ShapeDtypeStruct((qrows, features), jnp.bfloat16),
-            jax.ShapeDtypeStruct((8, features), jnp.float32),
+            jax.ShapeDtypeStruct((n, up8(nheads), HD), jnp.float32),
             jax.ShapeDtypeStruct((2 * rows_p, features), jnp.float32),
         ),
         in_specs=[hbm, hbm, hbm],
@@ -308,24 +337,28 @@
             pltpu.VMEM((slabs * rows_p, width), jnp.bfloat16),
             pltpu.VMEM((slabs * rows_p, width), jnp.bfloat16),
             pltpu.VMEM((n, qrows, width), jnp.bfloat16),
-            pltpu.VMEM((n, 8, width), jnp.float32),
+            pltpu.VMEM((n, up8(nheads), HD), jnp.float32),
             pltpu.VMEM((slabs, 2 * rows_p, width), jnp.float32),
             pltpu.VMEM((slabs, 2 * rows_p, width), jnp.bfloat16),
-            pltpu.VMEM((8, width), jnp.float32),
+            pltpu.VMEM((up8(2 * nheads), HD), jnp.float32),
             pltpu.VMEM((ndoc, n, 2 * rows_p, width), jnp.bfloat16),
-            pltpu.VMEM((ndoc, 8, width), jnp.float32),
+            pltpu.VMEM((ndoc, up8(2 * nheads), HD), jnp.float32),
             pltpu.VMEM((n, 2 * rows_p, width), jnp.float32),
-            pltpu.VMEM((n, 2 * rows_p, width), jnp.float32),
+            pltpu.VMEM((n, 2 * rows_p, width), jnp.bfloat16),
+            pltpu.VMEM((up8(2 * nheads), HD), jnp.float32),
+            pltpu.VMEM((n, 2 * rows_p, width), jnp.bfloat16),
+            pltpu.VMEM((n, up8(2 * nheads), HD), jnp.float32),
             dma((n,)), dma((n,)), dma((n,)), dma((n,)), dma((n,)), dma((n,)),
             dma((ndoc,)), dma((ndoc,)), dma((n,)), dma((n,)), dma((n,)), dma((n,)),
             dma((ndoc,)), dma((ndoc,)), dma((ndoc,)), dma((ndoc,)), dma((n,)), dma((n,)),
+            dma((n,)), dma((n,)),
         ],
         compiler_params=pltpu.CompilerParams(
             collective_id=0, has_side_effects=True, vmem_limit_bytes=58 * 1024 * 1024),
         cost_estimate=pl.CostEstimate(
             flops=16 * pairs, bytes_accessed=8 * qrows * features, transcendentals=pairs // HD),
     )(queries[0], out_grad[0], kv)
-    gq = decode(gq, gqp[0:1])
+    gq = decode(gq, gqp[:, :nheads].reshape(1, features))
     return gq[None], gkv[None, :rows], gkv[None, rows_p:rows_p + rows]
 
 

time: 63.9 us -> 62.2 us (0.973)
  the two profiles are of different devices: /device:TPU:25 before, /device:TPU:0 now
where the time goes in v3:
time: 62.2 us; the launch traced here: 60.9 us
  Pallas kernels  53 us (85%)
  other arithmetic  5.67 us (9%)
  local copies, waits for them, and re-layouts  1.68 us (3%)
  between operations  0.64 us (1%)
    pallas_call x1, Pallas kernels, shards(): pl.pallas_call(functools.partial(kernel, n, ndoc, rows, rows_p), out_shap...  53 us
    broadcast_in_dim x1, other arithmetic, shards(): return (gq[None], gkv[None, :rows], gkv[None, rows_p:rows_p + rows])  3.37 us
    broadcast_in_dim x1, local copies, waits for them, and re-layouts, shards(): return (gq[None], gkv[None, :rows], gkv[None, rows_p:rows_p + rows])  1.68 us
    concatenate x1, other arithmetic, shards(): jnp.concatenate([jnp.pad(mem_keys[0], pad), jnp.pad(mem_values[0], pad)],...  1.54 us

profile of v3, /device:TPU:0, one launch (start us, length us, event | category | flops | bytes accessed | tf_op | source)
XLA Modules:
  0.0 60.9 jit_solution(10586091318096571605)
XLA Ops:
  0.6 1.5 %pad_maximum_fusion.kv_ref = bf16[16,4096]{1,0:T(8,128)(2,1)} fusion(bf16[8,4096]{1,0:T(8,128)(2,1)} %bitcast.12, bf16[8,4096]{1,0:T(8,128)(2,1)} %bitcast.13), kind=kLoop, calls=%fused_computation.9 | loop fusion | flops 262144 | bytes 262144 | tf_op jit(solution)/shard_map/concatenate | solution.py:319
  2.2 53.0 %shard_map.67 = (bf16[128,4096]{1,0:T(8,128)(2,1)}, f32[8,8,128]{2,1,0:T(8,128)}, f32[16,4096]{1,0:T(8,128)}) custom-call(bf16[128,4096]{1,0:T(8,128)(2,1)} %bitcast.14, bf16[128,4096]{1,0:T(8,128)(2,1)} %bitcast.15, bf16[16,4096]{1,0:T(8,128)(2,1)} %pad_maximum_fusion.kv_ref), custom_call_target="tpu_custom_call" | custom-call | flops 2147483648 | bytes 4194304 | tf_op jit(solution)/shard_map/pallas_call | solution.py:324
  55.1 0.8 %slice_multiply_fusion = f32[8,4,128]{2,1,0:T(4,128)S(1)} fusion(f32[8,8,128]{2,1,0:T(8,128)} %get-tuple-element.7), kind=kLoop, calls=%fused_computation.12 | loop fusion | flops 4096 | bytes 32768 | tf_op jit(solution)/shard_map/mul | solution.py:55
  55.9 1.7 %slice_bitcast_fusion = (f32[1,8,4096]{2,1,0:T(8,128)}, f32[1,8,4096]{2,1,0:T(8,128)}) fusion(f32[16,4096]{1,0:T(8,128)} %get-tuple-element.8), kind=kLoop, calls=%fused_computation.10 | loop fusion | bytes 524288 | tf_op jit(solution)/shard_map/broadcast_in_dim | solution.py:362
  57.6 3.4 %fusion.4 = f32[1,128,4096]{2,1,0:T(8,128)} fusion(bf16[128,4096]{1,0:T(8,128)(2,1)} %get-tuple-element.6, f32[4096]{0:T(1024)S(1)} %bitcast.11), kind=kLoop, calls=%fused_computation.8 | loop fusion | flops 4194304 | bytes 3162112 | tf_op jit(solution)/shard_map/broadcast_in_dim | solution.py:362

commit v4 on v3

--- a/solution.py
+++ b/solution.py
@@ -70,12 +70,17 @@
 ):
     c = lax.axis_index("ctx")
     d = lax.axis_index("doc")
-    width = qbuf.shape[2]
+    halves, part_w = qbuf.shape[0], qbuf.shape[3]
+    width = halves * part_w
     nheads = width // HD
+    few = part_w // HD
     total = ndoc * n * rows_p
 
     def cols(i):
         return pl.ds(pl.multiple_of(i * width, width), width)
+
+    def part_cols(i, a):
+        return pl.ds(pl.multiple_of(i * width + a * part_w, part_w), part_w)
 
     barrier = pltpu.get_barrier_semaphore()
 
@@ -94,15 +99,15 @@
             src_ref=kv_ref.at[:, cols(p)], dst_ref=kvbuf.at[d * n + c],
             send_sem=kvs.at[p], recv_sem=kvr.at[c], device_id=(d, p), device_id_type=MESH)
 
-    def q_send(p):
-        return pltpu.make_async_remote_copy(
-            src_ref=q_ref.at[:, cols(p)], dst_ref=qbuf.at[c],
-            send_sem=qs.at[p], recv_sem=qr.at[c], device_id=(d, p), device_id_type=MESH)
-
-    def g_send(p):
-        return pltpu.make_async_remote_copy(
-            src_ref=g_ref.at[:, cols(p)], dst_ref=gbuf.at[c],
-            send_sem=gs.at[p], recv_sem=gr.at[c], device_id=(d, p), device_id_type=MESH)
+    def q_send(p, a):
+        return pltpu.make_async_remote_copy(
+            src_ref=q_ref.at[:, part_cols(p, a)], dst_ref=qbuf.at[a, c],
+            send_sem=qs.at[a * n + p], recv_sem=qr.at[a * n + c], device_id=(d, p), device_id_type=MESH)
+
+    def g_send(p, a):
+        return pltpu.make_async_remote_copy(
+            src_ref=g_ref.at[:, part_cols(p, a)], dst_ref=gbuf.at[a, c],
+            send_sem=gs.at[a * n + p], recv_sem=gr.at[a * n + c], device_id=(d, p), device_id_type=MESH)
 
     def z_send(t):
         return pltpu.make_async_remote_copy(
@@ -110,26 +115,26 @@
             send_sem=zs.at[t], recv_sem=zr.at[t],
             device_id=(lax.rem(d + t, ndoc), c), device_id_type=MESH)
 
-    def o_send(p):
-        return pltpu.make_async_remote_copy(
-            src_ref=gqbuf.at[p], dst_ref=gq_out.at[:, cols(c)],
-            send_sem=os.at[p], recv_sem=orr.at[c], device_id=(d, p), device_id_type=MESH)
+    def o_send(p, a):
+        return pltpu.make_async_remote_copy(
+            src_ref=gqbuf.at[a, p], dst_ref=gq_out.at[:, part_cols(c, a)],
+            send_sem=os.at[a * n + p], recv_sem=orr.at[a * n + c], device_id=(d, p), device_id_type=MESH)
 
     def p_send(p):
         return pltpu.make_async_remote_copy(
             src_ref=gqp.at[p], dst_ref=gqp_out.at[c],
             send_sem=ps.at[p], recv_sem=pr.at[c], device_id=(d, p), device_id_type=MESH)
 
-    def r_send(t):
+    def r_send(t, a):
         to = lax.rem(d + t, ndoc)
         return pltpu.make_async_remote_copy(
-            src_ref=part.at[pl.ds(to * n, n)], dst_ref=rsbuf.at[t],
-            send_sem=rs.at[t], recv_sem=rr.at[t], device_id=(to, c), device_id_type=MESH)
-
-    def t_send(t):
-        return pltpu.make_async_remote_copy(
-            src_ref=partp, dst_ref=rspbuf.at[t],
-            send_sem=ts.at[t], recv_sem=tr.at[t],
+            src_ref=part.at[a, pl.ds(to * n, n)], dst_ref=rsbuf.at[a, t],
+            send_sem=rs.at[a * ndoc + t], recv_sem=rr.at[a * ndoc + t], device_id=(to, c), device_id_type=MESH)
+
+    def t_send(t, a):
+        return pltpu.make_async_remote_copy(
+            src_ref=partp.at[a], dst_ref=rspbuf.at[a, t],
+            send_sem=ts.at[a * ndoc + t], recv_sem=tr.at[a * ndoc + t],
             device_id=(lax.rem(d + t, ndoc), c), device_id_type=MESH)
 
     def f_send(p):
@@ -144,33 +149,33 @@
 
     lower = lax.broadcasted_iota(jnp.int32, (2 * rows_p, HD), 0) < rows_p
 
-    def note_peaks(tile, x):
-        for first, half in ((0, x[:, :rows_p]), (nheads, x[:, rows_p:])):
-            peak = peak_of(half.reshape(-1, width), 0)
-            for h in range(nheads):
-                tile[first + h:first + h + 1] = peak[:, h * HD:(h + 1) * HD]
-
-    def spread(tile):
+    def peaks_of(x):
+        count = x.shape[2] // HD
+        tops = [peak_of(half.reshape(-1, x.shape[2]), 0) for half in (x[:, :rows_p], x[:, rows_p:])]
+        return [top[:, h * HD:(h + 1) * HD] for top in tops for h in range(count)]
+
+    def spread(tile, count):
         return jnp.concatenate(
-            [jnp.where(lower, tile[h:h + 1], tile[nheads + h:nheads + h + 1]) for h in range(nheads)], axis=1)
+            [jnp.where(lower, tile[h:h + 1], tile[count + h:count + h + 1]) for h in range(count)], axis=1)
 
     kv_own = pltpu.make_async_copy(kv_ref.at[:, cols(c)], kvbuf.at[d * n + c], kvr.at[c])
-    q_own = pltpu.make_async_copy(q_ref.at[:, cols(c)], qbuf.at[c], qr.at[c])
-    g_own = pltpu.make_async_copy(g_ref.at[:, cols(c)], gbuf.at[c], gr.at[c])
     kv_own.start()
 
     @pl.loop(1, n)
     def _(s):
         kv_send(partner(c, s, n)).start()
 
-    q_own.start()
-    g_own.start()
-
-    @pl.loop(1, n)
-    def _(s):
-        p = partner(c, s, n)
-        q_send(p).start()
-        g_send(p).start()
+    for a in range(halves):
+        pltpu.make_async_copy(q_ref.at[:, part_cols(c, a)], qbuf.at[a, c], qr.at[a * n + c]).start()
+    for a in range(halves):
+        pltpu.make_async_copy(g_ref.at[:, part_cols(c, a)], gbuf.at[a, c], gr.at[a * n + c]).start()
+
+    for a in range(halves):
+        @pl.loop(1, n)
+        def _(s, a=a):
+            p = partner(c, s, n)
+            q_send(p, a).start()
+            g_send(p, a).start()
 
     @pl.loop(0, n)
     def _(i):
@@ -197,13 +202,14 @@
 
     scale = HD ** (-0.5)
 
-    def step(s, carry):
+    def step(a, s, carry):
         p = source(c, s, n)
-        pltpu.make_async_copy(qbuf.at[p], qbuf.at[p], qr.at[p]).wait()
-        pltpu.make_async_copy(gbuf.at[p], gbuf.at[p], gr.at[p]).wait()
-        for h in range(nheads):
-            at = slice(h * HD, (h + 1) * HD)
-            q, g = qbuf[p, :, at], gbuf[p, :, at]
+        pltpu.make_async_copy(qbuf.at[a, p], qbuf.at[a, p], qr.at[a * n + p]).wait()
+        pltpu.make_async_copy(gbuf.at[a, p], gbuf.at[a, p], gr.at[a * n + p]).wait()
+        for h in range(few):
+            near = slice(h * HD, (h + 1) * HD)
+            at = slice(a * part_w + h * HD, a * part_w + (h + 1) * HD)
+            q, g = qbuf[a, p, :, near], gbuf[a, p, :, near]
             k, v = keys[:, at], values[:, at]
             expo = jnp.exp(dot(k, q, NT) * scale)
             if rows_p != rows:
@@ -218,8 +224,8 @@
             pr_hi, pr_lo = split16(prob)
             grad_q = dot(ds_hi, k, TN) + dot(ds_lo, k, TN)
             peak = peak_of(grad_q, 0)
-            gqp[p, h:h + 1] = peak
-            gqbuf[p, :, at] = encode(grad_q, peak)
+            gqp[p, a * few + h:a * few + h + 1] = peak
+            gqbuf[a, p, :, near] = encode(grad_q, peak)
             grad_k = dot(ds_hi, q, NN) + dot(ds_lo, q, NN)
             grad_v = dot(pr_hi, g, NN) + dot(pr_lo, g, NN)
             acc[:, :rows_p, at] += grad_k.reshape(ndoc * n, rows_p, HD)
@@ -227,37 +233,45 @@
 
         @pl.when(s > 0)
         def _():
-            o_send(p).start()
-            p_send(p).start()
+            o_send(p, a).start()
+            if a == halves - 1:
+                p_send(p).start()
 
         return carry
 
-    lax.fori_loop(0, n, step, 0)
-
-    note_peaks(partp, acc[...])
-    peaks = spread(partp[...])
-
-    @pl.loop(1, ndoc)
-    def _(t):
-        to = pl.ds(lax.rem(d + t, ndoc) * n, n)
-        part[to] = encode(acc[to], peaks[None])
-        t_send(t).start()
-        r_send(t).start()
-
-    gq_own = pltpu.make_async_copy(gqbuf.at[c], gq_out.at[:, cols(c)], orr.at[c])
-    gq_own.start()
+    for a in range(halves):
+        lax.fori_loop(0, n, functools.partial(step, a), 0)
+        chosen = slice(a * part_w, (a + 1) * part_w)
+        tops = peaks_of(acc[:, :, chosen])
+        for i, top in enumerate(tops):
+            partp[a, i:i + 1] = top
+        peaks = spread(partp[a], few)
+
+        @pl.loop(1, ndoc)
+        def _(t, a=a, chosen=chosen, peaks=peaks):
+            to = pl.ds(lax.rem(d + t, ndoc) * n, n)
+            part[a, to] = encode(acc[to, :, chosen], peaks[None])
+            t_send(t, a).start()
+            r_send(t, a).start()
+
+        pltpu.make_async_copy(gqbuf.at[a, c], gq_out.at[:, part_cols(c, a)], orr.at[a * n + c]).start()
+
     gqp_own = pltpu.make_async_copy(gqp.at[c], gqp_out.at[c], pr.at[c])
     gqp_own.start()
     fin_src[...] = acc[pl.ds(d * n, n)]
 
-    @pl.loop(1, ndoc)
-    def _(t):
-        t_send(t).wait_recv()
-        r_send(t).wait_recv()
-        fin_src[...] += decode(rsbuf[t], spread(rspbuf[t])[None])
-
-    note_peaks(finp, fin_src[...])
-    fin_enc[...] = encode(fin_src[...], spread(finp[...])[None])
+    for a in range(halves):
+        chosen = slice(a * part_w, (a + 1) * part_w)
+
+        @pl.loop(1, ndoc)
+        def _(t, a=a, chosen=chosen):
+            t_send(t, a).wait_recv()
+            r_send(t, a).wait_recv()
+            fin_src[:, :, chosen] += decode(rsbuf[a, t], spread(rspbuf[a, t], few)[None])
+
+    for i, top in enumerate(peaks_of(fin_src[...])):
+        finp[i:i + 1] = top
+    fin_enc[...] = encode(fin_src[...], spread(finp[...], nheads)[None])
 
     @pl.loop(1, n)
     def _(s):
@@ -276,12 +290,13 @@
 
     for i in range(n):
         at = slice(i * width, (i + 1) * width)
-        gkv_out[:, at] = decode(fin[i], spread(fin_peaks[i]))
+        gkv_out[:, at] = decode(fin[i], spread(fin_peaks[i], nheads))
 
     @pl.loop(0, n)
     def _(i):
-        mine = gq_out.at[:, cols(i)]
-        pltpu.make_async_copy(mine, mine, orr.at[i]).wait()
+        for a in range(halves):
+            mine = gq_out.at[:, part_cols(i, a)]
+            pltpu.make_async_copy(mine, mine, orr.at[a * n + i]).wait()
         peaks_in = gqp_out.at[i]
         pltpu.make_async_copy(peaks_in, peaks_in, pr.at[i]).wait()
 
@@ -289,9 +304,10 @@
     def _(s):
         p = partner(c, s, n)
         kv_send(p).wait_send()
-        q_send(p).wait_send()
-        g_send(p).wait_send()
-        o_send(p).wait_send()
+        for a in range(halves):
+            q_send(p, a).wait_send()
+            g_send(p, a).wait_send()
+            o_send(p, a).wait_send()
         p_send(p).wait_send()
         f_send(p).wait_send()
         u_send(p).wait_send()
@@ -299,8 +315,9 @@
     @pl.loop(1, ndoc)
     def _(t):
         z_send(t).wait_send()
-        r_send(t).wait_send()
-        t_send(t).wait_send()
+        for a in range(halves):
+            r_send(t, a).wait_send()
+            t_send(t, a).wait_send()
 
 
 def up8(x):
@@ -315,6 +332,8 @@
     width = features // n
     nheads = width // HD
     slabs = ndoc * n
+    halves = 2 if nheads % 2 == 0 else 1
+    few = nheads // halves
     pad = ((0, rows_p - rows), (0, 0))
     kv = jnp.concatenate([jnp.pad(mem_keys[0], pad), jnp.pad(mem_values[0], pad)], axis=0)
     dma = pltpu.SemaphoreType.DMA
@@ -331,27 +350,26 @@
         in_specs=[hbm, hbm, hbm],
         out_specs=(vmem, vmem, vmem),
         scratch_shapes=[
-            pltpu.VMEM((n, qrows, width), jnp.bfloat16),
-            pltpu.VMEM((n, qrows, width), jnp.bfloat16),
+            pltpu.VMEM((halves, n, qrows, width // halves), jnp.bfloat16),
+            pltpu.VMEM((halves, n, qrows, width // halves), jnp.bfloat16),
             pltpu.VMEM((slabs, 2 * rows_p, width), jnp.bfloat16),
             pltpu.VMEM((slabs * rows_p, width), jnp.bfloat16),
             pltpu.VMEM((slabs * rows_p, width), jnp.bfloat16),
-            pltpu.VMEM((n, qrows, width), jnp.bfloat16),
+            pltpu.VMEM((halves, n, qrows, width // halves), jnp.bfloat16),
             pltpu.VMEM((n, up8(nheads), HD), jnp.float32),
             pltpu.VMEM((slabs, 2 * rows_p, width), jnp.float32),
-            pltpu.VMEM((slabs, 2 * rows_p, width), jnp.bfloat16),
-            pltpu.VMEM((up8(2 * nheads), HD), jnp.float32),
-            pltpu.VMEM((ndoc, n, 2 * rows_p, width), jnp.bfloat16),
-            pltpu.VMEM((ndoc, up8(2 * nheads), HD), jnp.float32),
+            pltpu.VMEM((halves, slabs, 2 * rows_p, width // halves), jnp.bfloat16),
+            pltpu.VMEM((halves, up8(2 * few), HD), jnp.float32),
+            pltpu.VMEM((halves, ndoc, n, 2 * rows_p, width // halves), jnp.bfloat16),
+            pltpu.VMEM((halves, ndoc, up8(2 * few), HD), jnp.float32),
             pltpu.VMEM((n, 2 * rows_p, width), jnp.float32),
             pltpu.VMEM((n, 2 * rows_p, width), jnp.bfloat16),
             pltpu.VMEM((up8(2 * nheads), HD), jnp.float32),
             pltpu.VMEM((n, 2 * rows_p, width), jnp.bfloat16),
             pltpu.VMEM((n, up8(2 * nheads), HD), jnp.float32),
-            dma((n,)), dma((n,)), dma((n,)), dma((n,)), dma((n,)), dma((n,)),
-            dma((ndoc,)), dma((ndoc,)), dma((n,)), dma((n,)), dma((n,)), dma((n,)),
-            dma((ndoc,)), dma((ndoc,)), dma((ndoc,)), dma((ndoc,)), dma((n,)), dma((n,)),
-            dma((n,)), dma((n,)),
+            dma((n,)), dma((n,)), *[dma((halves * n,))] * 4,
+            dma((ndoc,)), dma((ndoc,)), dma((halves * n,)), dma((halves * n,)), dma((n,)), dma((n,)),
+            *[dma((halves * ndoc,))] * 4, dma((n,)), dma((n,)), dma((n,)), dma((n,)),
         ],
         compiler_params=pltpu.CompilerParams(
             collective_id=0, has_side_effects=True, vmem_limit_bytes=58 * 1024 * 1024),

time: 62.2 us -> 58.9 us (0.947); the launches traced: 60.9 us -> 58.6 us
  Pallas kernels: 53 us -> 50.6 us
    pallas_call x1, Pallas kernels: 53 us -> 50.6 us  [shards(): pl.pallas_call(functools.partial(kernel, n, ndoc, rows, rows_p), out_shap...]
where the time goes in v4:
time: 58.9 us; the launch traced here: 58.6 us
  Pallas kernels  50.6 us (86%)
  other arithmetic  5.67 us (10%)
  local copies, waits for them, and re-layouts  1.68 us (3%)
  between operations  0.64 us (1%)
    pallas_call x1, Pallas kernels, shards(): pl.pallas_call(functools.partial(kernel, n, ndoc, rows, rows_p), out_shap...  50.6 us
    broadcast_in_dim x1, other arithmetic, shards(): return (gq[None], gkv[None, :rows], gkv[None, rows_p:rows_p + rows])  3.37 us
    broadcast_in_dim x1, local copies, waits for them, and re-layouts, shards(): return (gq[None], gkv[None, :rows], gkv[None, rows_p:rows_p + rows])  1.68 us
    concatenate x1, other arithmetic, shards(): jnp.concatenate([jnp.pad(mem_keys[0], pad), jnp.pad(mem_values[0], pad)],...  1.54 us

profile of v4, /device:TPU:0, one launch (start us, length us, event | category | flops | bytes accessed | tf_op | source)
XLA Modules:
  0.0 58.6 jit_solution(12933657340845266099)
XLA Ops:
  0.6 1.5 %pad_maximum_fusion.kv_ref = bf16[16,4096]{1,0:T(8,128)(2,1)} fusion(bf16[8,4096]{1,0:T(8,128)(2,1)} %bitcast.12, bf16[8,4096]{1,0:T(8,128)(2,1)} %bitcast.13), kind=kLoop, calls=%fused_computation.9 | loop fusion | flops 262144 | bytes 262144 | tf_op jit(solution)/shard_map/concatenate | solution.py:338
  2.2 50.6 %shard_map.67 = (bf16[128,4096]{1,0:T(8,128)(2,1)}, f32[8,8,128]{2,1,0:T(8,128)}, f32[16,4096]{1,0:T(8,128)}) custom-call(bf16[128,4096]{1,0:T(8,128)(2,1)} %bitcast.14, bf16[128,4096]{1,0:T(8,128)(2,1)} %bitcast.15, bf16[16,4096]{1,0:T(8,128)(2,1)} %pad_maximum_fusion.kv_ref), custom_call_target="tpu_custom_call" | custom-call | flops 2147483648 | bytes 4194304 | tf_op jit(solution)/shard_map/pallas_call | solution.py:343
  52.8 0.8 %slice_multiply_fusion = f32[8,4,128]{2,1,0:T(4,128)S(1)} fusion(f32[8,8,128]{2,1,0:T(8,128)} %get-tuple-element.7), kind=kLoop, calls=%fused_computation.12 | loop fusion | flops 4096 | bytes 32768 | tf_op jit(solution)/shard_map/mul | solution.py:55
  53.5 1.7 %slice_bitcast_fusion = (f32[1,8,4096]{2,1,0:T(8,128)}, f32[1,8,4096]{2,1,0:T(8,128)}) fusion(f32[16,4096]{1,0:T(8,128)} %get-tuple-element.8), kind=kLoop, calls=%fused_computation.10 | loop fusion | bytes 524288 | tf_op jit(solution)/shard_map/broadcast_in_dim | solution.py:380
  55.2 3.4 %fusion.4 = f32[1,128,4096]{2,1,0:T(8,128)} fusion(bf16[128,4096]{1,0:T(8,128)(2,1)} %get-tuple-element.6, f32[4096]{0:T(1024)S(1)} %bitcast.11), kind=kLoop, calls=%fused_computation.8 | loop fusion | flops 4194304 | bytes 3162112 | tf_op jit(solution)/shard_map/broadcast_in_dim | solution.py:380

commit v5 on v4

--- a/solution.py
+++ b/solution.py
@@ -332,7 +332,7 @@
     width = features // n
     nheads = width // HD
     slabs = ndoc * n
-    halves = 2 if nheads % 2 == 0 else 1
+    halves = max(i for i in (1, 2, 4) if nheads % i == 0)
     few = nheads // halves
     pad = ((0, rows_p - rows), (0, 0))
     kv = jnp.concatenate([jnp.pad(mem_keys[0], pad), jnp.pad(mem_values[0], pad)], axis=0)

time: 58.9 us -> 62.6 us (1.063)
  Pallas kernels: 50.6 us -> 54.3 us
    pallas_call x1, Pallas kernels: 50.6 us -> 54.3 us  [shards(): pl.pallas_call(functools.partial(kernel, n, ndoc, rows, rows_p), out_shap...]
where the time goes in v5:
time: 62.6 us; the launch traced here: 62.3 us
  Pallas kernels  54.3 us (87%)
  other arithmetic  5.67 us (9%)
  local copies, waits for them, and re-layouts  1.68 us (3%)
  between operations  0.64 us (1%)
    pallas_call x1, Pallas kernels, shards(): pl.pallas_call(functools.partial(kernel, n, ndoc, rows, rows_p), out_shap...  54.3 us
    broadcast_in_dim x1, other arithmetic, shards(): return (gq[None], gkv[None, :rows], gkv[None, rows_p:rows_p + rows])  3.37 us
    broadcast_in_dim x1, local copies, waits for them, and re-layouts, shards(): return (gq[None], gkv[None, :rows], gkv[None, rows_p:rows_p + rows])  1.68 us
    concatenate x1, other arithmetic, shards(): jnp.concatenate([jnp.pad(mem_keys[0], pad), jnp.pad(mem_values[0], pad)],...  1.54 us

profile of v5, /device:TPU:0, one launch (start us, length us, event | category | flops | bytes accessed | tf_op | source)
XLA Modules:
  0.0 62.3 jit_solution(5356834297083677520)
XLA Ops:
  0.6 1.5 %pad_maximum_fusion.kv_ref = bf16[16,4096]{1,0:T(8,128)(2,1)} fusion(bf16[8,4096]{1,0:T(8,128)(2,1)} %bitcast.12, bf16[8,4096]{1,0:T(8,128)(2,1)} %bitcast.13), kind=kLoop, calls=%fused_computation.9 | loop fusion | flops 262144 | bytes 262144 | tf_op jit(solution)/shard_map/concatenate | solution.py:338
  2.2 54.3 %shard_map.67 = (bf16[128,4096]{1,0:T(8,128)(2,1)}, f32[8,8,128]{2,1,0:T(8,128)}, f32[16,4096]{1,0:T(8,128)}) custom-call(bf16[128,4096]{1,0:T(8,128)(2,1)} %bitcast.14, bf16[128,4096]{1,0:T(8,128)(2,1)} %bitcast.15, bf16[16,4096]{1,0:T(8,128)(2,1)} %pad_maximum_fusion.kv_ref), custom_call_target="tpu_custom_call" | custom-call | flops 2147483648 | bytes 4194304 | tf_op jit(solution)/shard_map/pallas_call | solution.py:343
  56.5 0.8 %slice_multiply_fusion = f32[8,4,128]{2,1,0:T(4,128)S(1)} fusion(f32[8,8,128]{2,1,0:T(8,128)} %get-tuple-element.7), kind=kLoop, calls=%fused_computation.12 | loop fusion | flops 4096 | bytes 32768 | tf_op jit(solution)/shard_map/mul | solution.py:55
  57.3 1.7 %slice_bitcast_fusion = (f32[1,8,4096]{2,1,0:T(8,128)}, f32[1,8,4096]{2,1,0:T(8,128)}) fusion(f32[16,4096]{1,0:T(8,128)} %get-tuple-element.8), kind=kLoop, calls=%fused_computation.10 | loop fusion | bytes 524288 | tf_op jit(solution)/shard_map/broadcast_in_dim | solution.py:380
  58.9 3.4 %fusion.4 = f32[1,128,4096]{2,1,0:T(8,128)} fusion(bf16[128,4096]{1,0:T(8,128)(2,1)} %get-tuple-element.6, f32[4096]{0:T(1024)S(1)} %bitcast.11), kind=kLoop, calls=%fused_computation.8 | loop fusion | flops 4194304 | bytes 3162112 | tf_op jit(solution)/shard_map/broadcast_in_dim | solution.py:380
